TPU v7x, 32 devices: a whole 2x2x4 slice. The times are simulated.
32 devices in a mesh: dp: 4 (over y, core), cent: 8 (over z, x).
Axes of the slice: x: 2, y: 2, z: 4, core: 2. Of those that a mesh axis runs over, the one named last changes fastest.
Arguments:
- fragments: bfloat16 [8192, 1024], P(('dp', 'cent')), may hold values from -1500 to 1500
- order: int32 [32, 256], P(('dp', 'cent')), may hold values from 0 to 255, each once within a row
- group_ids: int32 [8192, 1], P(('dp', 'cent')), may hold values from 0 to 7; in each aligned block of 256 rows (0 to 255, 256 to 511, ...) at most 64 rows name the same one
- w_first: bfloat16 [1024, 1024], replicated, may hold values from -0.1875 to 0.1875
- w_second: bfloat16 [1024, 256], replicated, may hold values from -0.1875 to 0.1875
- centroids: float32 [8192, 256], P('cent'), may hold values from -24 to 24
Outputs:
- centroids_out: float32 [8192, 256], P('cent')
Inputs may be any that keep to these rules, and one draw needn't show every extreme that they name: `order`: each row is a permutation of 0 to 255. `group_ids`: among the rows of one device (aligned blocks of 256 rows) no group is named by more than 64 rows, a bound that some block reaches.
All inputs are finite; a program needn't handle non-finite values.
Results may differ from a plain program's by a relative error of at most 0.0075.
Values may be sent and summed in bfloat16 or wider, within the bound.
A program may use at most 64 MiB of HBM per device.

v0:
```python
import jax
import jax.numpy as jnp
from jax import lax
from jax.sharding import PartitionSpec as P

STEPS = 2
beta_scale = 0.0625
prior_weight = 1.0
eps_value = 1e-05


def per_device(fragments, order, group_ids, w_first, w_second, centroids):
    rows_here = fragments.shape[0]
    picked = jnp.take(fragments, order[0], axis=0)
    hidden = jax.nn.gelu(
        jnp.dot(picked, w_first, preferred_element_type=jnp.float32), approximate=True
    ).astype(jnp.bfloat16)
    proj = jnp.dot(hidden, w_second, preferred_element_type=jnp.float32)
    total_rows = float(rows_here * lax.axis_size("dp") * lax.axis_size("cent"))
    mean = lax.psum(jnp.sum(proj, axis=0), ("dp", "cent")) / total_rows
    var = lax.psum(jnp.sum((proj - mean) ** 2, axis=0), ("dp", "cent")) / total_rows
    zrows = ((proj - mean) * lax.rsqrt(var + eps_value)).astype(jnp.bfloat16)
    width = zrows.shape[1]
    groups = group_ids[:, 0]
    group_count = lax.axis_size("cent")
    capacity = 2 * rows_here // group_count
    member = (groups[:, None] == jnp.arange(group_count, dtype=jnp.int32)[None, :]).astype(
        jnp.float32
    )
    index = jnp.arange(rows_here, dtype=jnp.int32)
    before = (index[:, None] > index[None, :]).astype(jnp.float32)
    rank = jnp.sum(jnp.dot(before, member) * member, axis=1).astype(jnp.int32)
    slot = groups * capacity + rank
    place = (slot[:, None] == jnp.arange(group_count * capacity, dtype=jnp.int32)[None, :]).astype(
        jnp.bfloat16
    )
    packed = lax.dot_general(
        place, zrows, (((0,), (0,)), ((), ())), preferred_element_type=jnp.float32
    ).astype(jnp.bfloat16)
    filled = jnp.sum(place.astype(jnp.float32), axis=0).astype(jnp.bfloat16)
    received, live = (
        lax.all_to_all(
            packed.reshape(group_count, capacity, width),
            "cent",
            split_axis=0,
            concat_axis=0,
            tiled=True,
        ),
        lax.all_to_all(
            filled.reshape(group_count, capacity), "cent", split_axis=0, concat_axis=0, tiled=True
        ),
    )
    received = received.reshape(group_count * capacity, width)
    live_rows = live.reshape(group_count * capacity).astype(jnp.float32)
    current = centroids
    parts_dp = lax.axis_size("dp")
    where_dp = lax.axis_index("dp")
    for step in range(STEPS):
        rounded = current.astype(jnp.bfloat16)
        cnorm = jnp.sum(current * current, axis=1)
        cross = lax.dot_general(
            received, rounded, (((1,), (1,)), ((), ())), preferred_element_type=jnp.float32
        )
        scores = beta_scale * (2.0 * cross - cnorm[None, :])
        top = jnp.max(scores, axis=1, keepdims=True)
        expo = jnp.exp(scores - top)
        resp = (expo / jnp.sum(expo, axis=1, keepdims=True) * live_rows[:, None]).astype(
            jnp.bfloat16
        )
        num = lax.dot_general(
            resp, received, (((0,), (0,)), ((), ())), preferred_element_type=jnp.float32
        )
        den = jnp.sum(resp.astype(jnp.float32), axis=0)
        share = current.shape[0] // parts_dp
        num_part, den_part = (
            lax.psum_scatter(num, "dp", scatter_dimension=0, tiled=True),
            lax.psum_scatter(den, "dp", scatter_dimension=0, tiled=True),
        )
        old = lax.dynamic_slice_in_dim(current, where_dp * share, share, 0)
        fresh = (num_part + prior_weight * old) / (den_part + prior_weight)[:, None]
        current = lax.all_gather(fresh, "dp", axis=0, tiled=True)
    return current


def solution(mesh):
    return jax.shard_map(
        per_device,
        mesh=mesh,
        in_specs=(
            P(("dp", "cent"), None),
            P(("dp", "cent"), None),
            P(("dp", "cent"), None),
            P(),
            P(),
            P("cent", None),
        ),
        out_specs=P("cent", None),
        check_vma=False,
    )
```

profile of v0, /device:TPU:0, one launch (start us, length us, event | category | flops | bytes accessed | tf_op | source)
XLA Modules:
  0.0 222.9 jit_solution(5794457838258072373)
XLA Ops:
  6.5 0.0 copy-start
  6.5 1.0 fusion.2
  7.6 0.7 multiply_add_fusion
  8.3 0.1 fusion.23
  8.4 0.7 all_to_all.12
  9.1 7.3 %all-to-all-start.1 = ((bf16[8,1,64]{2,1,0:T(2,128)(2,1)}), bf16[8,1,64]{2,1,0:T(2,128)(2,1)S(1)}, u32[]{:S(2)}, u32[]{:S(2)}) async-start(bf16[8,1,64]{2,1,0:T(2,128)(2,1)} %all_to_all.12), calls=%async_computation.1 | async-start | bytes 8192 | tf_op jit(solution)/shard_map/all_to_all | solution.py:49
  16.3 0.7 compare_select_fusion
  17.0 0.7 compare_and_fusion
  17.7 3.5 %gather_fusion = bf16[256,1024]{1,0:T(8,128)(2,1)} fusion(bf16[256,1024]{1,0:T(8,128)(2,1)} %param.6, s32[1024]{0:T(1024)S(1)} %pad_clamp_fusion), kind=kCustom, calls=%fused_computation | custom fusion | bytes 1049600 | tf_op jit(solution)/shard_map/jit(_take)/gather | solution.py:14
  21.2 0.0 copy-done
  21.2 0.0 copy-start.1
  21.2 2.4 %fusion.36 = (f32[256]{0:T(256)S(1)}, f32[256,256]{1,0:T(8,128)S(1)}) fusion(bf16[1024,256]{1,0:T(8,128)(2,1)} %param.10, bf16[1024,1024]{1,0:T(8,128)(2,1)S(1)} %copy-done, bf16[256,1024]{1,0:T(8,128)(2,1)} %gather_fusion, pred[256]{0:T(512)(128)(4,1)S(1)} %compare_and_fusion), kind=kOutput, calls=%fused_computation.60 | convolution fusion | flops 673775360 | bytes 3409152 | tf_op jit(solution)/shard_map/dot_general | solution.py:18
  23.6 40.8 %psum.14 = f32[256]{0:T(256)S(1)} all-reduce(f32[256]{0:T(256)S(1)} %get-tuple-element.9), channel_id=1, replica_groups=mesh['dp'=4,'cent'=8] {'dp','cent'}, use_global_device_ids=true, to_apply=%region_2.3 | all-reduce | flops 256 | bytes 2048 | tf_op jit(solution)/shard_map/psum | solution.py:20
  64.5 0.1 multiply_reduce_fusion.2
  64.5 40.0 %psum.15 = f32[256]{0:T(256)S(1)} all-reduce(f32[256]{0:T(256)S(1)} %multiply_reduce_fusion.2), channel_id=1, replica_groups=mesh['dp'=4,'cent'=8] {'dp','cent'}, use_global_device_ids=true, to_apply=%region_4.5 | all-reduce | flops 256 | bytes 2048 | tf_op jit(solution)/shard_map/psum | solution.py:21
  104.6 1.1 convolution_convert_fusion
  105.7 0.0 all-to-all-done.1
  105.7 5.3 %all-to-all-start = ((bf16[8,64,256]{2,1,0:T(8,128)(2,1)}), bf16[8,64,256]{2,1,0:T(8,128)(2,1)S(1)}, u32[]{:S(2)}, u32[]{:S(2)}) async-start(bf16[8,64,256]{2,1,0:T(8,128)(2,1)} %bitcast.22), calls=%async_computation | async-start | bytes 524288 | tf_op jit(solution)/shard_map/all_to_all | solution.py:42
  111.0 0.0 reduce-scatter.3.cloned.1.call-start
  111.0 0.0 copy-done.1
  111.1 0.2 multiply_reduce_fusion.1
  111.3 0.1 reshape.73
  111.4 7.9 %all-to-all-done = bf16[8,64,256]{2,1,0:T(8,128)(2,1)S(1)} async-done(((bf16[8,64,256]{2,1,0:T(8,128)(2,1)}), bf16[8,64,256]{2,1,0:T(8,128)(2,1)S(1)}, u32[]{:S(2)}, u32[]{:S(2)}) %all-to-all-start) | async-done | bytes 262176 | tf_op jit(solution)/shard_map/all_to_all | solution.py:42
  119.3 0.6 fusion.39
  119.9 0.5 fusion
  120.4 0.6 convert_reduce_fusion.1
  121.0 0.0 copy-start.2
  121.0 1.5 fusion.41
  122.5 0.0 reduce-scatter.3.cloned.1.call-update
  122.5 0.0 all-gather.3.cloned.1.call-start
  122.6 0.0 copy-done.2
  122.6 0.6 dynamic-slice
  123.8 5.7 %all-reduce = f32[1024]{0:T(1024)S(1)} all-reduce(f32[1024]{0:T(1024)S(1)} %get-tuple-element.7), channel_id=3, replica_groups=mesh['dp'=4,'cent'=8] {'dp'}, use_global_device_ids=true, to_apply=%region_11.12.clone | all-reduce | flops 1024 | bytes 8192
  129.5 0.1 dynamic-slice_add_fusion.1
  129.6 16.2 %reduce-scatter.3.cloned.1.call-done = f32[256,256]{1,0:T(8,128)} async-done(((f32[1024,256]{1,0:T(8,128)}), f32[256,256]{1,0:T(8,128)}) %reduce-scatter.3.cloned.1.call-update) | async-done | bytes 262160 | tf_op jit(solution)/shard_map/reduce_scatter | solution.py:76
  145.8 1.8 add_divide_fusion.1
  147.6 0.0 all-gather.3.cloned.1.call-update
  147.6 0.0 reduce-scatter.5.cloned.1.call-start
  147.6 16.8 %all-gather.3.cloned.1.call-done = f32[1024,256]{1,0:T(8,128)} async-done(((f32[256,256]{1,0:T(8,128)}), f32[1024,256]{1,0:T(8,128)}) %all-gather.3.cloned.1.call-update) | async-done | bytes 1048592 | tf_op jit(solution)/shard_map/all_gather | solution.py:81
  164.5 1.4 multiply_reduce_fusion
  165.9 1.8 fusion.40
  167.7 0.5 fusion.1
  168.2 0.6 convert_reduce_fusion
  168.9 1.5 fusion.42
  170.3 0.0 reduce-scatter.5.cloned.1.call-update
  170.3 0.0 all-gather.5.cloned.1.call-start
  170.4 5.9 %all-reduce.1 = f32[1024]{0:T(1024)S(1)} all-reduce(f32[1024]{0:T(1024)S(1)} %get-tuple-element.5), channel_id=5, replica_groups=mesh['dp'=4,'cent'=8] {'dp'}, use_global_device_ids=true, to_apply=%region_17.18.clone | all-reduce | flops 1024 | bytes 8192
  176.3 0.1 dynamic-slice_add_fusion
  176.4 19.0 %reduce-scatter.5.cloned.1.call-done = f32[256,256]{1,0:T(8,128)} async-done(((f32[1024,256]{1,0:T(8,128)}), f32[256,256]{1,0:T(8,128)}) %reduce-scatter.5.cloned.1.call-update) | async-done | bytes 262160 | tf_op jit(solution)/shard_map/reduce_scatter | solution.py:76
  195.4 1.8 add_divide_fusion
  197.2 0.0 all-gather.5.cloned.1.call-update
  197.3 16.9 %all-gather.5.cloned.1.call-done = f32[1024,256]{1,0:T(8,128)} async-done(((f32[256,256]{1,0:T(8,128)}), f32[1024,256]{1,0:T(8,128)}) %all-gather.5.cloned.1.call-update) | async-done | bytes 1048592 | tf_op jit(solution)/shard_map/all_gather | solution.py:81
  214.1 2.3 %copy.10 = f32[1024,256]{1,0:T(8,128)} copy(f32[1024,256]{1,0:T(8,128)} %all-gather.5.cloned.1.call-done) | data formatting | bytes 2097152
  (5 shorter events, 0.0 us)
Async XLA Ops:
  6.5 14.7 %copy-start = (bf16[1024,1024]{1,0:T(8,128)(2,1)S(1)}, bf16[1024,1024]{1,0:T(8,128)(2,1)}, u32[]{:S(2)}) copy-start(bf16[1024,1024]{1,0:T(8,128)(2,1)} %param.9) | copy-start | bytes 6291460
  9.1 96.6 %all-to-all-start.1 = ((bf16[8,1,64]{2,1,0:T(2,128)(2,1)}), bf16[8,1,64]{2,1,0:T(2,128)(2,1)S(1)}, u32[]{:S(2)}, u32[]{:S(2)}) async-start(bf16[8,1,64]{2,1,0:T(2,128)(2,1)} %all_to_all.12), calls=%async_computation.1 | async-start | bytes 8192 | tf_op jit(solution)/shard_map/all_to_all | solution.py:49
  21.2 89.9 %copy-start.1 = (f32[1024,256]{1,0:T(8,128)S(1)}, f32[1024,256]{1,0:T(8,128)}, u32[]{:S(2)}) copy-start(f32[1024,256]{1,0:T(8,128)} %param.11) | copy-start | bytes 3145732
  105.7 13.6 %all-to-all-start = ((bf16[8,64,256]{2,1,0:T(8,128)(2,1)}), bf16[8,64,256]{2,1,0:T(8,128)(2,1)S(1)}, u32[]{:S(2)}, u32[]{:S(2)}) async-start(bf16[8,64,256]{2,1,0:T(8,128)(2,1)} %bitcast.22), calls=%async_computation | async-start | bytes 524288 | tf_op jit(solution)/shard_map/all_to_all | solution.py:42
  111.0 34.8 %reduce-scatter.3.cloned.1.call-start = ((), (), s32[]{:S(2)}) async-start(), calls=%async_computation.4 | async-start | bytes 1310720 | tf_op jit(solution)/shard_map/reduce_scatter | solution.py:76
  121.0 1.5 copy-start.2
  122.5 42.0 %all-gather.3.cloned.1.call-start = ((), (), s32[]{:S(2)}) async-start(), calls=%async_computation.5 | async-start | bytes 1310720 | tf_op jit(solution)/shard_map/all_gather | solution.py:81
  147.6 47.8 %reduce-scatter.5.cloned.1.call-start = ((), (), s32[]{:S(2)}) async-start(), calls=%async_computation.6 | async-start | bytes 1310720 | tf_op jit(solution)/shard_map/reduce_scatter | solution.py:76
  170.3 43.8 %all-gather.5.cloned.1.call-start = ((), (), s32[]{:S(2)}) async-start(), calls=%async_computation.7 | async-start | bytes 1310720 | tf_op jit(solution)/shard_map/all_gather | solution.py:81
Sparse Core Ops, SparseCore 0:
  122.6 23.1 reduce-scatter.2
  147.7 16.7 all-gather.2
  170.5 24.8 reduce-scatter.4
  197.4 16.7 all-gather.4
where the time goes:
time: 224 us; the launch traced here: 223 us
  blocking collectives  92.4 us (41%)
  waiting for transfers between devices  77 us (34%)
  between operations  13.9 us (6%)
  starting transfers between devices  12.7 us (6%)
  other arithmetic  9.96 us (4%)
  matrix products  9.85 us (4%)
  local copies, waits for them, and re-layouts  7.14 us (3%)
    psum x1, blocking collectives, per_device(): mean = lax.psum(jnp.sum(proj, axis=0), ('dp', 'cent')) / total_rows  40.8 us
    psum x1, blocking collectives, per_device(): lax.psum(jnp.sum((proj - mean) ** 2, axis=0), ('dp', 'cent')) / total_rows  40 us
    reduce_scatter x2, waiting for transfers between devices, per_device(): lax.psum_scatter(num, 'dp', scatter_dimension=0, tiled=True)  35.3 us
    all_gather x2, waiting for transfers between devices, per_device(): current = lax.all_gather(fresh, 'dp', axis=0, tiled=True)  33.7 us
    unnamed x2, blocking collectives  11.6 us
    all_to_all x1, waiting for transfers between devices, per_device(): lax.all_to_all(packed.reshape(group_count, capacity, width), 'cent', spli...  7.92 us
    all_to_all x1, starting transfers between devices, per_device(): lax.all_to_all(filled.reshape(group_count, capacity), 'cent', split_axis=...  7.25 us
    all_to_all x1, starting transfers between devices, per_device(): lax.all_to_all(packed.reshape(group_count, capacity, width), 'cent', spli...  5.31 us
  transfers between devices with their start and end apart: 6, of which 5 were waited for; matrix products, arithmetic and copies ran while one was open for 4% of the time, Pallas kernels for 0%

commit v1 on v0

--- a/solution.py
+++ b/solution.py
@@ -17,7 +17,7 @@
     ).astype(jnp.bfloat16)
     proj = jnp.dot(hidden, w_second, preferred_element_type=jnp.float32)
     total_rows = float(rows_here * lax.axis_size("dp") * lax.axis_size("cent"))
-    mean = lax.psum(jnp.sum(proj, axis=0), ("dp", "cent")) / total_rows
+    mean = lax.psum(lax.psum(jnp.sum(proj, axis=0), "cent"), "dp") / total_rows
     var = lax.psum(jnp.sum((proj - mean) ** 2, axis=0), ("dp", "cent")) / total_rows
     zrows = ((proj - mean) * lax.rsqrt(var + eps_value)).astype(jnp.bfloat16)
     width = zrows.shape[1]

time: 224 us -> 208 us (0.929)
  blocking collectives: 92.4 us -> 76 us
    psum x1 -> x2, blocking collectives: 40.8 us -> 27.5 us  [per_device(): mean = lax.psum(lax.psum(jnp.sum(proj, axis=0), 'cent'), 'dp') / total_rows]
    psum x1, blocking collectives: 40 us -> 36.9 us  [per_device(): lax.psum(jnp.sum((proj - mean) ** 2, axis=0), ('dp', 'cent')) / total_rows]
  transfers between devices with their start and end apart: 6 -> 6, of which waited for: 5 -> 5; matrix products, arithmetic and copies ran while one was open for 4% -> 5% of each run, Pallas kernels for 0% -> 0%
where the time goes in v1:
time: 208 us; the launch traced here: 207 us
  waiting for transfers between devices  77.2 us (37%)
  blocking collectives  76 us (37%)
  between operations  13.9 us (7%)
  starting transfers between devices  13.3 us (6%)
  other arithmetic  9.96 us (5%)
  matrix products  9.86 us (5%)
  local copies, waits for them, and re-layouts  7.14 us (3%)
    psum x1, blocking collectives, per_device(): lax.psum(jnp.sum((proj - mean) ** 2, axis=0), ('dp', 'cent')) / total_rows  36.9 us
    reduce_scatter x2, waiting for transfers between devices, per_device(): lax.psum_scatter(num, 'dp', scatter_dimension=0, tiled=True)  35.3 us
    all_gather x2, waiting for transfers between devices, per_device(): current = lax.all_gather(fresh, 'dp', axis=0, tiled=True)  33.7 us
    psum x2, blocking collectives, per_device(): mean = lax.psum(lax.psum(jnp.sum(proj, axis=0), 'cent'), 'dp') / total_rows  27.5 us
    unnamed x2, blocking collectives  11.6 us
    all_to_all x1, waiting for transfers between devices, per_device(): lax.all_to_all(packed.reshape(group_count, capacity, width), 'cent', spli...  8.15 us
    all_to_all x1, starting transfers between devices, per_device(): lax.all_to_all(filled.reshape(group_count, capacity), 'cent', split_axis=...  7.25 us
    all_to_all x1, starting transfers between devices, per_device(): lax.all_to_all(packed.reshape(group_count, capacity, width), 'cent', spli...  5.89 us
  transfers between devices with their start and end apart: 6, of which 5 were waited for; matrix products, arithmetic and copies ran while one was open for 5% of the time, Pallas kernels for 0%

profile of v1, /device:TPU:0, one launch (start us, length us, event | category | flops | bytes accessed | tf_op | source)
XLA Modules:
  0.0 207.3 jit_solution(6757676710460142464)
XLA Ops:
  6.5 0.0 copy-start
  6.5 1.0 fusion.2
  7.6 0.7 multiply_add_fusion
  8.3 0.1 fusion.23
  8.4 0.7 all_to_all.12
  9.1 7.3 %all-to-all-start.1 = ((bf16[8,1,64]{2,1,0:T(2,128)(2,1)}), bf16[8,1,64]{2,1,0:T(2,128)(2,1)S(1)}, u32[]{:S(2)}, u32[]{:S(2)}) async-start(bf16[8,1,64]{2,1,0:T(2,128)(2,1)} %all_to_all.12), calls=%async_computation.1 | async-start | bytes 8192 | tf_op jit(solution)/shard_map/all_to_all | solution.py:49
  16.3 0.7 compare_select_fusion
  17.0 0.7 compare_and_fusion
  17.7 3.5 %gather_fusion = bf16[256,1024]{1,0:T(8,128)(2,1)} fusion(bf16[256,1024]{1,0:T(8,128)(2,1)} %param.6, s32[1024]{0:T(1024)S(1)} %pad_clamp_fusion), kind=kCustom, calls=%fused_computation | custom fusion | bytes 1049600 | tf_op jit(solution)/shard_map/jit(_take)/gather | solution.py:14
  21.2 0.0 copy-done
  21.2 0.0 copy-start.1
  21.2 2.4 %fusion.36 = (f32[256]{0:T(256)S(1)}, f32[256,256]{1,0:T(8,128)S(1)}) fusion(bf16[1024,256]{1,0:T(8,128)(2,1)} %param.10, bf16[1024,1024]{1,0:T(8,128)(2,1)S(1)} %copy-done, bf16[256,1024]{1,0:T(8,128)(2,1)} %gather_fusion, pred[256]{0:T(512)(128)(4,1)S(1)} %compare_and_fusion), kind=kOutput, calls=%fused_computation.60 | convolution fusion | flops 673775360 | bytes 3409152 | tf_op jit(solution)/shard_map/dot_general | solution.py:18
  23.6 21.8 %psum.21 = f32[256]{0:T(256)S(1)} all-reduce(f32[256]{0:T(256)S(1)} %get-tuple-element.9), channel_id=1, replica_groups=mesh['dp'=4,'cent'=8] {'cent'}, use_global_device_ids=true, to_apply=%region_2.3 | all-reduce | flops 256 | bytes 2048 | tf_op jit(solution)/shard_map/psum | solution.py:20
  45.5 5.6 %psum.22 = f32[256]{0:T(256)S(1)} all-reduce(f32[256]{0:T(256)S(1)} %psum.21), channel_id=1, replica_groups=mesh['dp'=4,'cent'=8] {'dp'}, use_global_device_ids=true, to_apply=%region_3.4 | all-reduce | flops 256 | bytes 2048 | tf_op jit(solution)/shard_map/psum | solution.py:20
  51.1 0.1 multiply_reduce_fusion.2
  51.2 36.9 %psum.23 = f32[256]{0:T(256)S(1)} all-reduce(f32[256]{0:T(256)S(1)} %multiply_reduce_fusion.2), channel_id=1, replica_groups=mesh['dp'=4,'cent'=8] {'dp','cent'}, use_global_device_ids=true, to_apply=%region_5.6 | all-reduce | flops 256 | bytes 2048 | tf_op jit(solution)/shard_map/psum | solution.py:21
  88.1 1.1 convolution_convert_fusion
  89.3 0.0 all-to-all-done.1
  89.3 5.9 %all-to-all-start = ((bf16[8,64,256]{2,1,0:T(8,128)(2,1)}), bf16[8,64,256]{2,1,0:T(8,128)(2,1)S(1)}, u32[]{:S(2)}, u32[]{:S(2)}) async-start(bf16[8,64,256]{2,1,0:T(8,128)(2,1)} %bitcast.22), calls=%async_computation | async-start | bytes 524288 | tf_op jit(solution)/shard_map/all_to_all | solution.py:42
  95.2 0.0 reduce-scatter.3.cloned.1.call-start
  95.2 0.0 copy-done.1
  95.2 0.2 multiply_reduce_fusion.1
  95.4 0.1 reshape.73
  95.5 8.1 %all-to-all-done = bf16[8,64,256]{2,1,0:T(8,128)(2,1)S(1)} async-done(((bf16[8,64,256]{2,1,0:T(8,128)(2,1)}), bf16[8,64,256]{2,1,0:T(8,128)(2,1)S(1)}, u32[]{:S(2)}, u32[]{:S(2)}) %all-to-all-start) | async-done | bytes 262176 | tf_op jit(solution)/shard_map/all_to_all | solution.py:42
  103.7 0.6 fusion.39
  104.2 0.5 fusion
  104.7 0.6 convert_reduce_fusion.1
  105.4 0.0 copy-start.2
  105.4 1.5 fusion.41
  106.8 0.0 reduce-scatter.3.cloned.1.call-update
  106.9 0.0 all-gather.3.cloned.1.call-start
  106.9 0.0 copy-done.2
  106.9 0.6 dynamic-slice
  108.2 5.7 %all-reduce = f32[1024]{0:T(1024)S(1)} all-reduce(f32[1024]{0:T(1024)S(1)} %get-tuple-element.7), channel_id=3, replica_groups=mesh['dp'=4,'cent'=8] {'dp'}, use_global_device_ids=true, to_apply=%region_12.13.clone | all-reduce | flops 1024 | bytes 8192
  113.9 0.1 dynamic-slice_add_fusion.1
  114.0 16.2 %reduce-scatter.3.cloned.1.call-done = f32[256,256]{1,0:T(8,128)} async-done(((f32[1024,256]{1,0:T(8,128)}), f32[256,256]{1,0:T(8,128)}) %reduce-scatter.3.cloned.1.call-update) | async-done | bytes 262160 | tf_op jit(solution)/shard_map/reduce_scatter | solution.py:76
  130.2 1.8 add_divide_fusion.1
  131.9 0.0 all-gather.3.cloned.1.call-update
  132.0 0.0 reduce-scatter.5.cloned.1.call-start
  132.0 16.8 %all-gather.3.cloned.1.call-done = f32[1024,256]{1,0:T(8,128)} async-done(((f32[256,256]{1,0:T(8,128)}), f32[1024,256]{1,0:T(8,128)}) %all-gather.3.cloned.1.call-update) | async-done | bytes 1048592 | tf_op jit(solution)/shard_map/all_gather | solution.py:81
  148.8 1.4 multiply_reduce_fusion
  150.3 1.8 fusion.40
  152.1 0.5 fusion.1
  152.6 0.6 convert_reduce_fusion
  153.2 1.5 fusion.42
  154.7 0.0 reduce-scatter.5.cloned.1.call-update
  154.7 0.0 all-gather.5.cloned.1.call-start
  154.7 5.9 %all-reduce.1 = f32[1024]{0:T(1024)S(1)} all-reduce(f32[1024]{0:T(1024)S(1)} %get-tuple-element.5), channel_id=5, replica_groups=mesh['dp'=4,'cent'=8] {'dp'}, use_global_device_ids=true, to_apply=%region_18.19.clone | all-reduce | flops 1024 | bytes 8192
  160.6 0.1 dynamic-slice_add_fusion
  160.7 19.0 %reduce-scatter.5.cloned.1.call-done = f32[256,256]{1,0:T(8,128)} async-done(((f32[1024,256]{1,0:T(8,128)}), f32[256,256]{1,0:T(8,128)}) %reduce-scatter.5.cloned.1.call-update) | async-done | bytes 262160 | tf_op jit(solution)/shard_map/reduce_scatter | solution.py:76
  179.7 1.8 add_divide_fusion
  181.6 0.0 all-gather.5.cloned.1.call-update
  181.6 16.9 %all-gather.5.cloned.1.call-done = f32[1024,256]{1,0:T(8,128)} async-done(((f32[256,256]{1,0:T(8,128)}), f32[1024,256]{1,0:T(8,128)}) %all-gather.5.cloned.1.call-update) | async-done | bytes 1048592 | tf_op jit(solution)/shard_map/all_gather | solution.py:81
  198.5 2.3 %copy.10 = f32[1024,256]{1,0:T(8,128)} copy(f32[1024,256]{1,0:T(8,128)} %all-gather.5.cloned.1.call-done) | data formatting | bytes 2097152
  (5 shorter events, 0.0 us)
Async XLA Ops:
  6.5 14.7 %copy-start = (bf16[1024,1024]{1,0:T(8,128)(2,1)S(1)}, bf16[1024,1024]{1,0:T(8,128)(2,1)}, u32[]{:S(2)}) copy-start(bf16[1024,1024]{1,0:T(8,128)(2,1)} %param.9) | copy-start | bytes 6291460
  9.1 80.2 %all-to-all-start.1 = ((bf16[8,1,64]{2,1,0:T(2,128)(2,1)}), bf16[8,1,64]{2,1,0:T(2,128)(2,1)S(1)}, u32[]{:S(2)}, u32[]{:S(2)}) async-start(bf16[8,1,64]{2,1,0:T(2,128)(2,1)} %all_to_all.12), calls=%async_computation.1 | async-start | bytes 8192 | tf_op jit(solution)/shard_map/all_to_all | solution.py:49
  21.2 74.0 %copy-start.1 = (f32[1024,256]{1,0:T(8,128)S(1)}, f32[1024,256]{1,0:T(8,128)}, u32[]{:S(2)}) copy-start(f32[1024,256]{1,0:T(8,128)} %param.11) | copy-start | bytes 3145732
  89.3 14.4 %all-to-all-start = ((bf16[8,64,256]{2,1,0:T(8,128)(2,1)}), bf16[8,64,256]{2,1,0:T(8,128)(2,1)S(1)}, u32[]{:S(2)}, u32[]{:S(2)}) async-start(bf16[8,64,256]{2,1,0:T(8,128)(2,1)} %bitcast.22), calls=%async_computation | async-start | bytes 524288 | tf_op jit(solution)/shard_map/all_to_all | solution.py:42
  95.2 35.0 %reduce-scatter.3.cloned.1.call-start = ((), (), s32[]{:S(2)}) async-start(), calls=%async_computation.4 | async-start | bytes 1310720 | tf_op jit(solution)/shard_map/reduce_scatter | solution.py:76
  105.4 1.5 copy-start.2
  106.9 42.0 %all-gather.3.cloned.1.call-start = ((), (), s32[]{:S(2)}) async-start(), calls=%async_computation.5 | async-start | bytes 1310720 | tf_op jit(solution)/shard_map/all_gather | solution.py:81
  132.0 47.8 %reduce-scatter.5.cloned.1.call-start = ((), (), s32[]{:S(2)}) async-start(), calls=%async_computation.6 | async-start | bytes 1310720 | tf_op jit(solution)/shard_map/reduce_scatter | solution.py:76
  154.7 43.8 %all-gather.5.cloned.1.call-start = ((), (), s32[]{:S(2)}) async-start(), calls=%async_computation.7 | async-start | bytes 1310720 | tf_op jit(solution)/shard_map/all_gather | solution.py:81
Sparse Core Ops, SparseCore 0:
  107.0 23.1 reduce-scatter.2
  132.1 16.6 all-gather.2
  154.8 24.8 reduce-scatter.4
  181.7 16.7 all-gather.4
